TPU v7x, 32 devices: a whole 2x2x4 slice. The times are simulated.
32 devices in a mesh: groups: 2 (over x), tm: 16 (over z, y, core).
Axes of the slice: x: 2, y: 2, z: 4, core: 2. Of those that a mesh axis runs over, the one named last changes fastest.
Arguments:
- sharded_latents: bfloat16 [32, 6144], P('groups', 'tm'), parts along dimension 0, may hold values from -6 to 6
- sample_frame_count: int32 [16], P('groups'), parts along dimension 0, may hold values from 5 to 8, as said below
- entry_kernel: bfloat16 [27, 16, 384], replicated, may hold values from -0.3125 to 0.3125
- entry_bias: float32 [384], replicated, may hold values from -3 to 3
- norm_scale_gain: float32 [384], replicated, may hold values from 0.25 to 1.75
- residual_kernel: bfloat16 [27, 384, 384], P(None, 'tm'), may hold values from -0.0625 to 0.0625
- residual_bias: float32 [384], replicated, may hold values from -3 to 3
Outputs:
- decoded: bfloat16 [128, 6, 16, 384], P(('groups', 'tm')), parts along dimension 0
There are 2 independent parts, one for each index of `groups`. A program takes and returns all parts, laid end to end along the dimension named above; an argument that names none is the same for every part. Nothing has to cross between parts.
Inputs may be any that keep to these rules, and one draw needn't show every extreme that they name: `sample_frame_count`: every sample has more than half of its 8 frames valid; some sample has all of them valid.
All inputs are finite; a program needn't handle non-finite values.
Results may differ from a plain program's by a relative error of at most 0.009.
Values may be sent and summed in bfloat16 or wider, within the bound.
A program may use at most 64 MiB of HBM per device.

v0:
```python
import jax
import jax.numpy as jnp
from jax import lax
from jax.sharding import PartitionSpec as P

LATENT_CHANNELS = 16
C = 384
PROMPT_SAMPLES = 8
BLOCK_FRAMES = 4
LATENT_ROWS = 6
LATENT_COLUMNS = 16


def from_behind(block, axis, distance):
    devices = range(lax.axis_size(axis))
    route = [(i - distance, i) for i in devices if i - distance in devices]
    return lax.ppermute(block, axis, route)


def causal_conv(frames, weight):
    frames_out = frames.shape[0] - 2
    inputs = frames.shape[3]
    padded = jnp.pad(frames, ((0, 0), (1, 1), (1, 1), (0, 0)))
    total = jnp.zeros((frames_out * LATENT_ROWS * LATENT_COLUMNS, weight.shape[2]), jnp.float32)
    for time_tap in range(3):
        for row_tap in range(3):
            for col_tap in range(3):
                window = padded[
                    time_tap : time_tap + frames_out,
                    row_tap : row_tap + LATENT_ROWS,
                    col_tap : col_tap + LATENT_COLUMNS,
                    :,
                ]
                window = window.reshape(frames_out * LATENT_ROWS * LATENT_COLUMNS, inputs)
                tap = 9 * time_tap + 3 * row_tap + col_tap
                total = total + jnp.dot(window, weight[tap], preferred_element_type=jnp.float32)
    return total


def activate(stream, norm_scale_gain):
    values = stream.astype(jnp.float32)
    scale = lax.rsqrt(jnp.mean(values * values, axis=-1, keepdims=True) + 1e-06)
    return jax.nn.silu(values * scale * norm_scale_gain).astype(jnp.bfloat16)


def to_cells(planes):
    return jnp.transpose(
        planes.reshape(planes.shape[0], LATENT_CHANNELS, LATENT_ROWS, LATENT_COLUMNS), (0, 2, 3, 1)
    )


def shards(
    sharded_latents,
    sample_frame_count,
    entry_kernel,
    entry_bias,
    norm_scale_gain,
    residual_kernel,
    residual_bias,
):
    gathered_latents = lax.all_to_all(
        sharded_latents, "tm", split_axis=0, concat_axis=1, tiled=True
    )
    latent_volume = gathered_latents.reshape(
        BLOCK_FRAMES, LATENT_CHANNELS, LATENT_ROWS * LATENT_COLUMNS
    )
    position = lax.axis_index("tm")
    block = position // PROMPT_SAMPLES
    sample = position % PROMPT_SAMPLES
    keep = block > 0
    earlier = from_behind(latent_volume, "tm", PROMPT_SAMPLES)
    earlier = jnp.where(keep, earlier, jnp.zeros_like(earlier))
    frames = to_cells(jnp.concatenate([earlier, latent_volume], axis=0))
    widened = (causal_conv(frames, entry_kernel) + entry_bias).astype(jnp.bfloat16)
    active_all = activate(widened, norm_scale_gain).reshape(
        BLOCK_FRAMES + 2, LATENT_ROWS, LATENT_COLUMNS, C
    )
    behind = jnp.where(keep, active_all[:2], jnp.zeros_like(active_all[:2]))
    extended = jnp.concatenate([behind, active_all[2:]], axis=0)
    stream = widened[2 * LATENT_ROWS * LATENT_COLUMNS :]
    kernel_all = lax.all_gather(residual_kernel, "tm", axis=1, tiled=True)
    branch = causal_conv(extended, kernel_all)
    total = (stream.astype(jnp.float32) + (branch + residual_bias)).reshape(
        BLOCK_FRAMES, LATENT_ROWS, LATENT_COLUMNS, C
    )
    limit = jnp.sum(jnp.where(jnp.arange(PROMPT_SAMPLES) == sample, sample_frame_count, 0))
    frame_index = block * BLOCK_FRAMES + jnp.arange(BLOCK_FRAMES)
    valid = (frame_index < limit)[:, None, None, None]
    return jnp.where(valid, total, jnp.zeros_like(total)).astype(jnp.bfloat16)


def solution(mesh):
    in_specs = (P("groups", "tm"), P("groups"), P(), P(), P(), P(None, "tm", None), P())
    out_specs = P(("groups", "tm"), None, None, None)
    return jax.shard_map(shards, mesh=mesh, in_specs=in_specs, out_specs=out_specs, check_vma=False)
```

profile of v0, /device:TPU:0, one launch (start us, length us, event | category | flops | bytes accessed | tf_op | source)
XLA Modules:
  0.0 109.1 jit_solution(9590959347050248216)
XLA Ops:
  7.8 1.4 %reduce.2 = bf16[16,384]{1,0:T(8,128)(2,1)S(1)} reduce(bf16[16,1,384]{2,0,1:T(8,128)(2,1)} %bitcast.334, bf16[]{:T(256)} %broadcast.36), dimensions={1}, to_apply=%copy.62.reduce_sub_computation | reduce | bytes 24578 | tf_op jit(solution)/shard_map/all_to_all | solution.py:61
  9.8 7.4 %all-to-all-start = ((bf16[16,2,192]{2,1,0:T(2,128)(2,1)}), bf16[16,2,192]{2,1,0:T(2,128)(2,1)S(1)}, u32[]{:S(2)}, u32[]{:S(2)}) async-start(bf16[16,2,192]{2,1,0:T(2,128)(2,1)} %reshape.257), calls=%async_computation | async-start | bytes 32768 | tf_op jit(solution)/shard_map/all_to_all | solution.py:61
  17.2 1.3 %fusion.70 = s32[]{:T(128)} fusion(s32[8]{0:T(128)} %param.8, s32[]{:T(128)S(6)} %select_n.39), kind=kLoop, calls=%fused_computation.186 | loop fusion | flops 23 | bytes 40 | tf_op jit(solution)/shard_map/reduce_sum | solution.py:86
  18.5 5.2 %all-to-all-done = bf16[16,2,192]{2,1,0:T(2,128)(2,1)S(1)} async-done(((bf16[16,2,192]{2,1,0:T(2,128)(2,1)}), bf16[16,2,192]{2,1,0:T(2,128)(2,1)S(1)}, u32[]{:S(2)}, u32[]{:S(2)}) %all-to-all-start) | async-done | bytes 12320 | tf_op jit(solution)/shard_map/all_to_all | solution.py:61
  24.0 2.4 %collective-permute-start = (bf16[4,16,96]{2,1,0:T(8,128)(2,1)S(1)}, bf16[4,16,96]{2,1,0:T(8,128)(2,1)S(1)}, u32[]{:S(2)}, u32[]{:S(2)}) collective-permute-start(bf16[4,16,96]{2,1,0:T(8,128)(2,1)S(1)} %reshape.200), channel_id=1, source_target_pairs={{0,8},{1,9},{2,10},{3,11},{4,12},{5,13},{6,14},{7,15},{16,24},{17,... | collective-permute-start | bytes 36872 | tf_op jit(solution)/shard_map/ppermute | solution.py:17
  28.5 0.8 reshape.201
  30.7 0.8 reshape.203
  32.4 0.8 reshape.205
  35.7 0.8 reshape.209
  38.7 0.8 reshape.212
  42.8 1.0 fusion.41
  43.8 1.0 convolution_add_fusion.25
  44.9 1.1 convolution_add_fusion.24
  54.5 0.9 fusion.13
  55.4 1.2 %pad_slice_fusion.1 = (bf16[4,6,16,384]{3,2,1,0:T(8,128)(2,1)}, bf16[4,6,16,384]{3,2,1,0:T(8,128)(2,1)}, bf16[4,6,16,384]{3,2,1,0:T(8,128)(2,1)}, bf16[4,6,16,384]{3,2,1,0:T(8,128)(2,1)}, bf16[4,6,16,384]{3,2,1,0:T(8,128)(2,1)}) fusion(bf16[6,6,16,384]{3,2,1,0:T(8,128)(2,1)S(1)} %pad_maximum_fusion), kind=kLoop, calls=%fused_computation.1 | loop fusion | bytes 1916928 | tf_op jit(solution)/shard_map/slice | solution.py:28
  56.6 2.2 %pad_slice_fusion = (bf16[4,6,16,384]{3,2,1,0:T(8,128)(2,1)}, bf16[4,6,16,384]{3,2,1,0:T(8,128)(2,1)}, bf16[4,6,16,384]{3,2,1,0:T(8,128)(2,1)}, bf16[4,6,16,384]...) fusion(bf16[6,6,16,384]{3,2,1,0:T(8,128)(2,1)S(1)} %pad_maximum, ...), kind=kLoop, calls=%fused_computation | loop fusion | bytes 6045696 | tf_op jit(solution)/shard_map/slice | solution.py:28
  58.8 26.1 %all-gather.2.cloned.1.call-done = bf16[27,384,384]{2,1,0:T(8,128)(2,1)} async-done(((bf16[27,24,384]{2,1,0:T(8,128)(2,1)}), bf16[27,384,384]{2,1,0:T(8,128)(2,1)}) %all-gather.2.cloned.1.call-update) | async-done | bytes 7962640 | tf_op jit(solution)/shard_map/all_gather | solution.py:81
  84.9 1.5 %fusion.14 = f32[384,384]{1,0:T(8,128)S(1)} fusion(bf16[384,384]{1,0:T(8,128)(2,1)} %bitcast.333, bf16[27,384,384]{2,1,0:T(8,128)(2,1)} %all-gather.2.cloned.1.call-done), kind=kOutput, calls=%fused_computation.125 | convolution fusion | flops 113246208 | bytes 1179648 | tf_op jit(solution)/shard_map/dot_general | solution.py:36
  86.5 2.0 %convolution_add_fusion.51 = f32[384,384]{1,0:T(8,128)S(1)} fusion(f32[384,384]{1,0:T(8,128)S(1)} %fusion.14, bf16[384,384]{1,0:T(8,128)(2,1)} %bitcast.324, bf16[27,384,384]{2,1,0:T(8,128)(2,1)} %all-gather.2.cloned.1.call-done), kind=kOutput, calls=%fused_computation.79 | convolution fusion | flops 113393664 | bytes 1769472 | tf_op jit(solution)/shard_map/dot_general | solution.py:36
  88.5 1.4 %convolution_add_fusion.50 = f32[384,384]{1,0:T(8,128)S(1)} fusion(f32[384,384]{1,0:T(8,128)S(1)} %convolution_add_fusion.51, bf16[384,384]{1,0:T(8,128)(2,1)} %bitcast.323, bf16[27,384,384]{2,1,0:T(8,128)(2,1)} %all-gather.2.cloned.1.call-done), kind=kOutput, calls=%fused_computation.78 | convolution fusion | flops 113393664 | bytes 1769472 | tf_op jit(solution)/shard_map/dot_general | solution.py:36
  89.9 1.4 %convolution_add_fusion.49 = f32[384,384]{1,0:T(8,128)S(1)} fusion(f32[384,384]{1,0:T(8,128)S(1)} %convolution_add_fusion.50, bf16[384,384]{1,0:T(8,128)(2,1)} %bitcast.322, bf16[27,384,384]{2,1,0:T(8,128)(2,1)} %all-gather.2.cloned.1.call-done), kind=kOutput, calls=%fused_computation.77 | convolution fusion | flops 113393664 | bytes 1769472 | tf_op jit(solution)/shard_map/dot_general | solution.py:36
  91.3 1.4 %convolution_add_fusion.48 = f32[384,384]{1,0:T(8,128)S(1)} fusion(f32[384,384]{1,0:T(8,128)S(1)} %convolution_add_fusion.49, bf16[384,384]{1,0:T(8,128)(2,1)} %bitcast.327, bf16[27,384,384]{2,1,0:T(8,128)(2,1)} %all-gather.2.cloned.1.call-done), kind=kOutput, calls=%fused_computation.76 | convolution fusion | flops 113393664 | bytes 1769472 | tf_op jit(solution)/shard_map/dot_general | solution.py:36
  92.7 1.3 %convolution_add_fusion.47 = f32[384,384]{1,0:T(8,128)S(1)} fusion(f32[384,384]{1,0:T(8,128)S(1)} %convolution_add_fusion.48, bf16[384,384]{1,0:T(8,128)(2,1)} %bitcast.321, bf16[27,384,384]{2,1,0:T(8,128)(2,1)S(1)} %copy-done), kind=kOutput, calls=%fused_computation.75 | convolution fusion | flops 113393664 | bytes 1769472 | tf_op jit(solution)/shard_map/dot_general | solution.py:36
  101.4 0.8 select_convert_fusion
  (165 shorter events, 29.7 us)
Async XLA Ops:
  6.5 78.4 %all-gather.2.cloned.1.call-start = ((), (), s32[]{:S(2)}) async-start(), calls=%async_computation.1 | async-start | bytes 8460288 | tf_op jit(solution)/shard_map/all_gather | solution.py:81
  9.8 13.9 %all-to-all-start = ((bf16[16,2,192]{2,1,0:T(2,128)(2,1)}), bf16[16,2,192]{2,1,0:T(2,128)(2,1)S(1)}, u32[]{:S(2)}, u32[]{:S(2)}) async-start(bf16[16,2,192]{2,1,0:T(2,128)(2,1)} %reshape.257), calls=%async_computation | async-start | bytes 32768 | tf_op jit(solution)/shard_map/all_to_all | solution.py:61
  24.0 3.9 %collective-permute-start = (bf16[4,16,96]{2,1,0:T(8,128)(2,1)S(1)}, bf16[4,16,96]{2,1,0:T(8,128)(2,1)S(1)}, u32[]{:S(2)}, u32[]{:S(2)}) collective-permute-start(bf16[4,16,96]{2,1,0:T(8,128)(2,1)S(1)} %reshape.200), channel_id=1, source_target_pairs={{0,8},{1,9},{2,10},{3,11},{4,12},{5,13},{6,14},{7,15},{16,24},{17,... | collective-permute-start | bytes 36872 | tf_op jit(solution)/shard_map/ppermute | solution.py:17
  37.8 8.2 %copy-start.13 = (bf16[576,16]{0,1:T(8,128)(2,1)S(1)}, bf16[576,16]{0,1:T(8,128)(2,1)}, u32[]{:S(2)}) copy-start(bf16[576,16]{0,1:T(8,128)(2,1)} %reshape.204) | copy-start | bytes 55300
  38.6 7.7 %copy-start.14 = (bf16[576,16]{0,1:T(8,128)(2,1)S(1)}, bf16[576,16]{0,1:T(8,128)(2,1)}, u32[]{:S(2)}) copy-start(bf16[576,16]{0,1:T(8,128)(2,1)} %reshape.205) | copy-start | bytes 55300
  38.7 4.1 %copy-start.12 = (bf16[27,16,384]{2,1,0:T(8,128)(2,1)S(1)}, bf16[27,16,384]{2,1,0:T(8,128)(2,1)}, u32[]{:S(2)}) copy-start(bf16[27,16,384]{2,1,0:T(8,128)(2,1)} %param.9) | copy-start | bytes 995332
  39.9 6.7 %copy-start.15 = (bf16[576,16]{0,1:T(8,128)(2,1)S(1)}, bf16[576,16]{0,1:T(8,128)(2,1)}, u32[]{:S(2)}) copy-start(bf16[576,16]{0,1:T(8,128)(2,1)} %reshape.206) | copy-start | bytes 55300
  40.6 6.4 %copy-start.16 = (bf16[576,16]{0,1:T(8,128)(2,1)S(1)}, bf16[576,16]{0,1:T(8,128)(2,1)}, u32[]{:S(2)}) copy-start(bf16[576,16]{0,1:T(8,128)(2,1)} %reshape.207) | copy-start | bytes 55300
  41.2 6.1 %copy-start.17 = (bf16[576,16]{0,1:T(8,128)(2,1)S(1)}, bf16[576,16]{0,1:T(8,128)(2,1)}, u32[]{:S(2)}) copy-start(bf16[576,16]{0,1:T(8,128)(2,1)} %reshape.208) | copy-start | bytes 55300
  41.9 5.7 %copy-start.18 = (bf16[576,16]{0,1:T(8,128)(2,1)S(1)}, bf16[576,16]{0,1:T(8,128)(2,1)}, u32[]{:S(2)}) copy-start(bf16[576,16]{0,1:T(8,128)(2,1)} %reshape.209) | copy-start | bytes 55300
  42.5 5.4 %copy-start.19 = (bf16[576,16]{0,1:T(8,128)(2,1)S(1)}, bf16[576,16]{0,1:T(8,128)(2,1)}, u32[]{:S(2)}) copy-start(bf16[576,16]{0,1:T(8,128)(2,1)} %reshape.210) | copy-start | bytes 55300
  43.8 4.4 %copy-start.20 = (bf16[576,16]{0,1:T(8,128)(2,1)S(1)}, bf16[576,16]{0,1:T(8,128)(2,1)}, u32[]{:S(2)}) copy-start(bf16[576,16]{0,1:T(8,128)(2,1)} %reshape.211) | copy-start | bytes 55300
  44.9 3.7 %copy-start.21 = (bf16[576,16]{0,1:T(8,128)(2,1)S(1)}, bf16[576,16]{0,1:T(8,128)(2,1)}, u32[]{:S(2)}) copy-start(bf16[576,16]{0,1:T(8,128)(2,1)} %reshape.212) | copy-start | bytes 55300
  50.8 3.2 %copy-start.23 = (f32[384]{0:T(512)S(1)}, f32[384]{0:T(512)}, u32[]{:S(2)}) copy-start(f32[384]{0:T(512)} %param.11) | copy-start | bytes 4612
  84.9 7.8 %copy-start = (bf16[27,384,384]{2,1,0:T(8,128)(2,1)S(1)}, bf16[27,384,384]{2,1,0:T(8,128)(2,1)}, u32[]{:S(2)}) copy-start(bf16[27,384,384]{2,1,0:T(8,128)(2,1)} %all-gather.2.cloned.1.call-done) | copy-start | bytes 23887876
  84.9 9.1 %copy-start.5 = (bf16[4,6,16,384]{3,2,1,0:T(8,128)(2,1)S(1)}, bf16[4,6,16,384]{3,2,1,0:T(8,128)(2,1)}, u32[]{:S(2)}) copy-start(bf16[4,6,16,384]{3,2,1,0:T(8,128)(2,1)} %get-tuple-element.10) | copy-start | bytes 884740
  84.9 9.5 %copy-start.4 = (bf16[4,6,16,384]{3,2,1,0:T(8,128)(2,1)S(1)}, bf16[4,6,16,384]{3,2,1,0:T(8,128)(2,1)}, u32[]{:S(2)}) copy-start(bf16[4,6,16,384]{3,2,1,0:T(8,128)(2,1)} %get-tuple-element.11) | copy-start | bytes 884740
  84.9 9.8 %copy-start.3 = (bf16[4,6,16,384]{3,2,1,0:T(8,128)(2,1)S(1)}, bf16[4,6,16,384]{3,2,1,0:T(8,128)(2,1)}, u32[]{:S(2)}) copy-start(bf16[4,6,16,384]{3,2,1,0:T(8,128)(2,1)} %get-tuple-element.12) | copy-start | bytes 884740
  84.9 10.2 %copy-start.2 = (bf16[4,6,16,384]{3,2,1,0:T(8,128)(2,1)S(1)}, bf16[4,6,16,384]{3,2,1,0:T(8,128)(2,1)}, u32[]{:S(2)}) copy-start(bf16[4,6,16,384]{3,2,1,0:T(8,128)(2,1)} %get-tuple-element.13) | copy-start | bytes 884740
  86.4 9.0 %copy-start.1 = (bf16[4,6,16,384]{3,2,1,0:T(8,128)(2,1)S(1)}, bf16[4,6,16,384]{3,2,1,0:T(8,128)(2,1)}, u32[]{:S(2)}) copy-start(bf16[4,6,16,384]{3,2,1,0:T(8,128)(2,1)} %get-tuple-element.14) | copy-start | bytes 884740
  91.3 5.2 %copy-start.7 = (bf16[4,6,16,384]{3,2,1,0:T(8,128)(2,1)S(1)}, bf16[4,6,16,384]{3,2,1,0:T(8,128)(2,1)}, u32[]{:S(2)}) copy-start(bf16[4,6,16,384]{3,2,1,0:T(8,128)(2,1)} %get-tuple-element.29) | copy-start | bytes 884740
  96.1 3.1 %copy-start.11 = (bf16[4,6,16,384]{3,2,1,0:T(8,128)(2,1)S(1)}, bf16[4,6,16,384]{3,2,1,0:T(8,128)(2,1)}, u32[]{:S(2)}) copy-start(bf16[4,6,16,384]{3,2,1,0:T(8,128)(2,1)} %get-tuple-element.25) | copy-start | bytes 884740
  96.8 3.1 %copy-start.10 = (bf16[4,6,16,384]{3,2,1,0:T(8,128)(2,1)S(1)}, bf16[4,6,16,384]{3,2,1,0:T(8,128)(2,1)}, u32[]{:S(2)}) copy-start(bf16[4,6,16,384]{3,2,1,0:T(8,128)(2,1)} %get-tuple-element.26) | copy-start | bytes 884740
  97.2 3.1 %copy-start.9 = (bf16[4,6,16,384]{3,2,1,0:T(8,128)(2,1)S(1)}, bf16[4,6,16,384]{3,2,1,0:T(8,128)(2,1)}, u32[]{:S(2)}) copy-start(bf16[4,6,16,384]{3,2,1,0:T(8,128)(2,1)} %get-tuple-element.27) | copy-start | bytes 884740
  (4 other events, 12.5 us)
Sparse Core Ops, SparseCore 0:
  9.5 75.3 all-gather.1
where the time goes:
time: 110 us; the launch traced here: 109 us
  waiting for transfers between devices  32.7 us (30%)
  matrix products  27 us (25%)
  local copies, waits for them, and re-layouts  19.7 us (18%)
  between operations  14.4 us (13%)
  starting transfers between devices  9.76 us (9%)
  other arithmetic  5.58 us (5%)
    dot_general x54, matrix products, causal_conv(): jnp.dot(window, weight[tap], preferred_element_type=jnp.float32)  27 us
    all_gather x1, waiting for transfers between devices, shards(): kernel_all = lax.all_gather(residual_kernel, 'tm', axis=1, tiled=True)  26.1 us
    reshape x27, local copies, waits for them, and re-layouts, causal_conv(): window = window.reshape(frames_out * LATENT_ROWS * LATENT_COLUMNS, inputs)  12 us
    all_to_all x1, starting transfers between devices, shards(): lax.all_to_all(sharded_latents, 'tm', split_axis=0, concat_axis=1, tiled=...  7.39 us
    slice x32, local copies, waits for them, and re-layouts, causal_conv(): padded[time_tap:time_tap + frames_out, row_tap:row_tap + LATENT_ROWS, col...  5.87 us
    all_to_all x1, waiting for transfers between devices, shards(): lax.all_to_all(sharded_latents, 'tm', split_axis=0, concat_axis=1, tiled=...  5.18 us
    ppermute x1, starting transfers between devices, from_behind(): return lax.ppermute(block, axis, route)  2.37 us
  transfers between devices with their start and end apart: 3, of which 3 were waited for; matrix products, arithmetic and copies ran while one was open for 32% of the time, Pallas kernels for 0%

commit v1 on v0

--- a/solution.py
+++ b/solution.py
@@ -2,6 +2,7 @@
 import jax.numpy as jnp
 from jax import lax
 from jax.sharding import PartitionSpec as P
+from jax.lax import axis_index, axis_size, ppermute
 
 LATENT_CHANNELS = 16
 C = 384
@@ -78,7 +79,34 @@
     behind = jnp.where(keep, active_all[:2], jnp.zeros_like(active_all[:2]))
     extended = jnp.concatenate([behind, active_all[2:]], axis=0)
     stream = widened[2 * LATENT_ROWS * LATENT_COLUMNS :]
-    kernel_all = lax.all_gather(residual_kernel, "tm", axis=1, tiled=True)
+    mid_arr = axis_size("tm")
+    x_now = axis_index("tm")
+    left_arr, t1, all_values = (mid_arr, x_now, residual_kernel.shape[1])
+    rack = []
+    for m in tuple(range(left_arr)):
+        rack.append((m, (m + 1) % left_arr))
+    heap = []
+    for m in [*range(left_arr)]:
+        heap.append((m, (m - 1) % left_arr))
+    kernel_all = jnp.zeros(
+        (*residual_kernel.shape[:1], left_arr * all_values, *residual_kernel.shape[2:]),
+        residual_kernel.dtype,
+    )
+    kernel_all = lax.dynamic_update_slice_in_dim(
+        kernel_all, residual_kernel, t1 * all_values, axis=1
+    )
+    e_now = passed = residual_kernel
+    front = left_arr // 2
+    for jj in tuple(range(1, front + 1)):
+        e_now = ppermute(e_now, perm=rack, axis_name="tm")
+        kernel_all = lax.dynamic_update_slice_in_dim(
+            kernel_all, e_now, (t1 - jj) % left_arr * all_values, axis=1
+        )
+        if jj < left_arr - front:
+            passed = ppermute(passed, axis_name="tm", perm=heap)
+            kernel_all = lax.dynamic_update_slice_in_dim(
+                kernel_all, passed, (t1 + jj) % left_arr * all_values, axis=1
+            )
     branch = causal_conv(extended, kernel_all)
     total = (stream.astype(jnp.float32) + (branch + residual_bias)).reshape(
         BLOCK_FRAMES, LATENT_ROWS, LATENT_COLUMNS, C

time: 110 us -> 202 us (1.84)
  the two profiles are of different devices: /device:TPU:0 before, /device:TPU:22 now
where the time goes in v1:
time: 202 us; the launch traced here: 200 us
  waiting for transfers between devices  66.3 us (33%)
  local copies, waits for them, and re-layouts  62.7 us (31%)
  matrix products  45 us (22%)
  starting transfers between devices  20.5 us (10%)
  other arithmetic  4.12 us (2%)
    ppermute x8, waiting for transfers between devices, shards(): e_now = ppermute(e_now, perm=rack, axis_name='tm')  52.8 us
    dot_general x54, matrix products, causal_conv(): jnp.dot(window, weight[tap], preferred_element_type=jnp.float32)  45 us
    reshape x27, local copies, waits for them, and re-layouts, causal_conv(): window = window.reshape(frames_out * LATENT_ROWS * LATENT_COLUMNS, inputs)  20.8 us
    slice x32, local copies, waits for them, and re-layouts, causal_conv(): padded[time_tap:time_tap + frames_out, row_tap:row_tap + LATENT_ROWS, col...  19.8 us
    ppermute x7, starting transfers between devices, shards(): passed = ppermute(passed, axis_name='tm', perm=heap)  12.8 us
    ppermute x7, waiting for transfers between devices, shards(): passed = ppermute(passed, axis_name='tm', perm=heap)  8.75 us
    dynamic_update_slice x8, local copies, waits for them, and re-layouts, shards(): lax.dynamic_update_slice_in_dim(kernel_all, e_now, (t1 - jj) % left_arr *...  7.98 us
    dynamic_update_slice x7, local copies, waits for them, and re-layouts, shards(): lax.dynamic_update_slice_in_dim(kernel_all, passed, (t1 + jj) % left_arr...  7.15 us
  transfers between devices with their start and end apart: 17, of which 12 were waited for; matrix products, arithmetic and copies ran while one was open for 37% of the time, Pallas kernels for 0%

profile of v1, /device:TPU:22, one launch (start us, length us, event | category | flops | bytes accessed | tf_op | source)
XLA Modules:
  0.0 199.8 jit_solution(17754596582333642749)
XLA Ops:
  0.0 1.7 collective-permute-start.2
  4.3 6.3 %all-to-all-start = ((bf16[16,2,192]{2,1,0:T(2,128)(2,1)}), bf16[16,2,192]{2,1,0:T(2,128)(2,1)S(1)}, u32[]{:S(2)}, u32[]{:S(2)}) async-start(bf16[16,2,192]{2,1,0:T(2,128)(2,1)} %reshape.257), calls=%async_computation | async-start | bytes 32768 | tf_op jit(solution)/shard_map/all_to_all | solution.py:62
  10.6 4.3 %broadcast_in_dim.33 = bf16[27,384,384]{2,1,0:T(8,128)(2,1)} broadcast(bf16[]{:T(256)} %constant.124.clone.1), dimensions={} | broadcast | bytes 7962626 | tf_op jit(solution)/shard_map/broadcast_in_dim | solution.py:91
  19.2 4.8 %collective-permute-done = bf16[4,16,96]{2,1,0:T(8,128)(2,1)S(1)} collective-permute-done((bf16[4,16,96]{2,1,0:T(8,128)(2,1)S(1)}, bf16[4,16,96]{2,1,0:T(8,128)(2,1)S(1)}, u32[]{:S(2)}, u32[]{:S(2)}) %collective-permute-start) | collective-permute-done | bytes 12320 | tf_op jit(solution)/shard_map/ppermute | solution.py:18
  28.6 1.7 reshape.202
  52.0 1.7 reshape.208
  72.8 1.8 collective-permute-start.4
  74.6 11.4 %collective-permute-done.3 = bf16[27,24,384]{2,1,0:T(8,128)(2,1)S(1)} collective-permute-done((bf16[27,24,384]{2,1,0:T(8,128)(2,1)}, bf16[27,24,384]{2,1,0:T(8,128)(2,1)S(1)}, u32[]{:S(2)}, u32[]{:S(2)}) %collective-permute-start.3) | collective-permute-done | bytes 497696 | tf_op jit(solution)/shard_map/ppermute | solution.py:101
  86.8 3.5 %collective-permute-done.4 = bf16[27,24,384]{2,1,0:T(8,128)(2,1)S(1)} collective-permute-done((bf16[27,24,384]{2,1,0:T(8,128)(2,1)}, bf16[27,24,384]{2,1,0:T(8,128)(2,1)S(1)}, u32[]{:S(2)}, u32[]{:S(2)}) %collective-permute-start.4) | collective-permute-done | bytes 497696 | tf_op jit(solution)/shard_map/ppermute | solution.py:106
  90.4 1.8 collective-permute-start.6
  92.2 7.5 %collective-permute-done.5 = bf16[27,24,384]{2,1,0:T(8,128)(2,1)S(1)} collective-permute-done((bf16[27,24,384]{2,1,0:T(8,128)(2,1)S(1)}, bf16[27,24,384]{2,1,0:T(8,128)(2,1)S(1)}, u32[]{:S(2)}, u32[]{:S(2)}) %collective-permute-start.5) | collective-permute-done | bytes 497696 | tf_op jit(solution)/shard_map/ppermute | solution.py:101
  100.0 3.6 %collective-permute-done.6 = bf16[27,24,384]{2,1,0:T(8,128)(2,1)S(1)} collective-permute-done((bf16[27,24,384]{2,1,0:T(8,128)(2,1)S(1)}, bf16[27,24,384]{2,1,0:T(8,128)(2,1)S(1)}, u32[]{:S(2)}, u32[]{:S(2)}) %collective-permute-start.6) | collective-permute-done | bytes 497696 | tf_op jit(solution)/shard_map/ppermute | solution.py:106
  103.6 1.9 collective-permute-start.8
  105.6 7.4 %collective-permute-done.7 = bf16[27,24,384]{2,1,0:T(8,128)(2,1)S(1)} collective-permute-done((bf16[27,24,384]{2,1,0:T(8,128)(2,1)S(1)}, bf16[27,24,384]{2,1,0:T(8,128)(2,1)S(1)}, u32[]{:S(2)}, u32[]{:S(2)}) %collective-permute-start.7) | collective-permute-done | bytes 497696 | tf_op jit(solution)/shard_map/ppermute | solution.py:101
  114.4 1.9 constant_dynamic-update-slice_fusion.14
  117.2 1.9 collective-permute-start.10
  119.2 1.9 constant_dynamic-update-slice_fusion.13
  121.0 5.6 %collective-permute-done.9 = bf16[27,24,384]{2,1,0:T(8,128)(2,1)S(1)} collective-permute-done((bf16[27,24,384]{2,1,0:T(8,128)(2,1)S(1)}, bf16[27,24,384]{2,1,0:T(8,128)(2,1)S(1)}, u32[]{:S(2)}, u32[]{:S(2)}) %collective-permute-start.9) | collective-permute-done | bytes 497696 | tf_op jit(solution)/shard_map/ppermute | solution.py:101
  130.0 1.9 collective-permute-start.12
  132.7 7.6 %collective-permute-done.11 = bf16[27,24,384]{2,1,0:T(8,128)(2,1)S(1)} collective-permute-done((bf16[27,24,384]{2,1,0:T(8,128)(2,1)S(1)}, bf16[27,24,384]{2,1,0:T(8,128)(2,1)S(1)}, u32[]{:S(2)}, u32[]{:S(2)}) %collective-permute-start.11) | collective-permute-done | bytes 497696 | tf_op jit(solution)/shard_map/ppermute | solution.py:101
  143.0 1.7 collective-permute-start.14
  145.6 8.4 %collective-permute-done.13 = bf16[27,24,384]{2,1,0:T(8,128)(2,1)S(1)} collective-permute-done((bf16[27,24,384]{2,1,0:T(8,128)(2,1)S(1)}, bf16[27,24,384]{2,1,0:T(8,128)(2,1)S(1)}, u32[]{:S(2)}, u32[]{:S(2)}) %collective-permute-start.13) | collective-permute-done | bytes 497696 | tf_op jit(solution)/shard_map/ppermute | solution.py:101
  157.5 4.8 %collective-permute-done.15 = bf16[27,24,384]{2,1,0:T(8,128)(2,1)S(1)} collective-permute-done((bf16[27,24,384]{2,1,0:T(8,128)(2,1)S(1)}, bf16[27,24,384]{2,1,0:T(8,128)(2,1)S(1)}, u32[]{:S(2)}, u32[]{:S(2)}) %collective-permute-start.15) | collective-permute-done | bytes 497696 | tf_op jit(solution)/shard_map/ppermute | solution.py:101
  197.0 1.9 fusion.28
  (195 shorter events, 101.5 us)
Async XLA Ops:
  0.0 14.9 %copy-start = (bf16[27,24,384]{2,1,0:T(8,128)(2,1)S(1)}, bf16[27,24,384]{2,1,0:T(8,128)(2,1)}, u32[]{:S(2)}) copy-start(bf16[27,24,384]{2,1,0:T(8,128)(2,1)} %param.12) | copy-start | bytes 1492996
  0.0 15.8 %copy-start.17 = (s32[8]{0:T(128)S(1)}, s32[8]{0:T(128)}, u32[]{:S(2)}) copy-start(s32[8]{0:T(128)} %param.8) | copy-start | bytes 100
  0.0 72.1 %collective-permute-start.1 = (bf16[27,24,384]{2,1,0:T(8,128)(2,1)}, bf16[27,24,384]{2,1,0:T(8,128)(2,1)}, u32[]{:S(2)}, u32[]{:S(2)}) collective-permute-start(bf16[27,24,384]{2,1,0:T(8,128)(2,1)} %param.12), channel_id=1, source_target_pairs={{0,1},{1,2},{2,3},{3,4},{4,5},{5,6},{6,7},{7,8},{8,9},{9,10},{10,1... | collective-permute-start | bytes 1493000 | tf_op jit(solution)/shard_map/ppermute | solution.py:101
  0.0 72.8 %collective-permute-start.2 = (bf16[27,24,384]{2,1,0:T(8,128)(2,1)}, bf16[27,24,384]{2,1,0:T(8,128)(2,1)}, u32[]{:S(2)}, u32[]{:S(2)}) collective-permute-start(bf16[27,24,384]{2,1,0:T(8,128)(2,1)} %param.12), channel_id=1, source_target_pairs={{0,15},{1,0},{2,1},{3,2},{4,3},{5,4},{6,5},{7,6},{8,7},{9,8},{10,9... | collective-permute-start | bytes 1493000 | tf_op jit(solution)/shard_map/ppermute | solution.py:106
  4.3 12.9 %all-to-all-start = ((bf16[16,2,192]{2,1,0:T(2,128)(2,1)}), bf16[16,2,192]{2,1,0:T(2,128)(2,1)S(1)}, u32[]{:S(2)}, u32[]{:S(2)}) async-start(bf16[16,2,192]{2,1,0:T(2,128)(2,1)} %reshape.257), calls=%async_computation | async-start | bytes 32768 | tf_op jit(solution)/shard_map/all_to_all | solution.py:62
  17.4 6.5 %collective-permute-start = (bf16[4,16,96]{2,1,0:T(8,128)(2,1)S(1)}, bf16[4,16,96]{2,1,0:T(8,128)(2,1)S(1)}, u32[]{:S(2)}, u32[]{:S(2)}) collective-permute-start(bf16[4,16,96]{2,1,0:T(8,128)(2,1)S(1)} %reshape.200), channel_id=1, source_target_pairs={{0,8},{1,9},{2,10},{3,11},{4,12},{5,13},{6,14},{7,15},{16,24},{17,... | collective-permute-start | bytes 36872 | tf_op jit(solution)/shard_map/ppermute | solution.py:18
  56.9 6.8 %copy-start.2 = (bf16[576,16]{0,1:T(8,128)(2,1)S(1)}, bf16[576,16]{0,1:T(8,128)(2,1)}, u32[]{:S(2)}) copy-start(bf16[576,16]{0,1:T(8,128)(2,1)} %reshape.202) | copy-start | bytes 55300
  56.9 7.2 %copy-start.3 = (bf16[576,16]{0,1:T(8,128)(2,1)S(1)}, bf16[576,16]{0,1:T(8,128)(2,1)}, u32[]{:S(2)}) copy-start(bf16[576,16]{0,1:T(8,128)(2,1)} %reshape.203) | copy-start | bytes 55300
  69.7 16.4 %copy-start.14 = (f32[384]{0:T(512)S(1)}, f32[384]{0:T(512)}, u32[]{:S(2)}) copy-start(f32[384]{0:T(512)} %param.10) | copy-start | bytes 4612
  70.0 16.5 %copy-start.15 = (f32[384]{0:T(512)S(1)}, f32[384]{0:T(512)}, u32[]{:S(2)}) copy-start(f32[384]{0:T(512)} %param.11) | copy-start | bytes 4612
  72.1 13.9 %collective-permute-start.3 = (bf16[27,24,384]{2,1,0:T(8,128)(2,1)}, bf16[27,24,384]{2,1,0:T(8,128)(2,1)S(1)}, u32[]{:S(2)}, u32[]{:S(2)}) collective-permute-start(bf16[27,24,384]{2,1,0:T(8,128)(2,1)} %collective-permute-done.1), channel_id=1, source_target_pairs={{0,1},{1,2},{2,3},{3,4},{4,5},{5,6},{6,7},{7,8},{8,9},{9,10},{10,1... | collective-permute-start | bytes 1493000 | tf_op jit(solution)/shard_map/ppermute | solution.py:101
  72.8 17.5 %collective-permute-start.4 = (bf16[27,24,384]{2,1,0:T(8,128)(2,1)}, bf16[27,24,384]{2,1,0:T(8,128)(2,1)S(1)}, u32[]{:S(2)}, u32[]{:S(2)}) collective-permute-start(bf16[27,24,384]{2,1,0:T(8,128)(2,1)} %collective-permute-done.2), channel_id=1, source_target_pairs={{0,15},{1,0},{2,1},{3,2},{4,3},{5,4},{6,5},{7,6},{8,7},{9,8},{10,9... | collective-permute-start | bytes 1493000 | tf_op jit(solution)/shard_map/ppermute | solution.py:106
  86.0 13.7 %collective-permute-start.5 = (bf16[27,24,384]{2,1,0:T(8,128)(2,1)S(1)}, bf16[27,24,384]{2,1,0:T(8,128)(2,1)S(1)}, u32[]{:S(2)}, u32[]{:S(2)}) collective-permute-start(bf16[27,24,384]{2,1,0:T(8,128)(2,1)S(1)} %collective-permute-done.3), channel_id=1, source_target_pairs={{0,1},{1,2},{2,3},{3,4},{4,5},{5,6},{6,7},{7,8},{8,9},{9,10},{10,1... | collective-permute-start | bytes 1493000 | tf_op jit(solution)/shard_map/ppermute | solution.py:101
  90.4 13.2 %collective-permute-start.6 = (bf16[27,24,384]{2,1,0:T(8,128)(2,1)S(1)}, bf16[27,24,384]{2,1,0:T(8,128)(2,1)S(1)}, u32[]{:S(2)}, u32[]{:S(2)}) collective-permute-start(bf16[27,24,384]{2,1,0:T(8,128)(2,1)S(1)} %collective-permute-done.4), channel_id=1, source_target_pairs={{0,15},{1,0},{2,1},{3,2},{4,3},{5,4},{6,5},{7,6},{8,7},{9,8},{10,9... | collective-permute-start | bytes 1493000 | tf_op jit(solution)/shard_map/ppermute | solution.py:106
  99.7 13.3 %collective-permute-start.7 = (bf16[27,24,384]{2,1,0:T(8,128)(2,1)S(1)}, bf16[27,24,384]{2,1,0:T(8,128)(2,1)S(1)}, u32[]{:S(2)}, u32[]{:S(2)}) collective-permute-start(bf16[27,24,384]{2,1,0:T(8,128)(2,1)S(1)} %collective-permute-done.5), channel_id=1, source_target_pairs={{0,1},{1,2},{2,3},{3,4},{4,5},{5,6},{6,7},{7,8},{8,9},{9,10},{10,1... | collective-permute-start | bytes 1493000 | tf_op jit(solution)/shard_map/ppermute | solution.py:101
  103.6 13.7 %collective-permute-start.8 = (bf16[27,24,384]{2,1,0:T(8,128)(2,1)S(1)}, bf16[27,24,384]{2,1,0:T(8,128)(2,1)S(1)}, u32[]{:S(2)}, u32[]{:S(2)}) collective-permute-start(bf16[27,24,384]{2,1,0:T(8,128)(2,1)S(1)} %collective-permute-done.6), channel_id=1, source_target_pairs={{0,15},{1,0},{2,1},{3,2},{4,3},{5,4},{6,5},{7,6},{8,7},{9,8},{10,9... | collective-permute-start | bytes 1493000 | tf_op jit(solution)/shard_map/ppermute | solution.py:106
  113.0 13.7 %collective-permute-start.9 = (bf16[27,24,384]{2,1,0:T(8,128)(2,1)S(1)}, bf16[27,24,384]{2,1,0:T(8,128)(2,1)S(1)}, u32[]{:S(2)}, u32[]{:S(2)}) collective-permute-start(bf16[27,24,384]{2,1,0:T(8,128)(2,1)S(1)} %collective-permute-done.7), channel_id=1, source_target_pairs={{0,1},{1,2},{2,3},{3,4},{4,5},{5,6},{6,7},{7,8},{8,9},{9,10},{10,1... | collective-permute-start | bytes 1493000 | tf_op jit(solution)/shard_map/ppermute | solution.py:101
  117.2 12.7 %collective-permute-start.10 = (bf16[27,24,384]{2,1,0:T(8,128)(2,1)S(1)}, bf16[27,24,384]{2,1,0:T(8,128)(2,1)S(1)}, u32[]{:S(2)}, u32[]{:S(2)}) collective-permute-start(bf16[27,24,384]{2,1,0:T(8,128)(2,1)S(1)} %collective-permute-done.8), channel_id=1, source_target_pairs={{0,15},{1,0},{2,1},{3,2},{4,3},{5,4},{6,5},{7,6},{8,7},{9,8},{10,9... | collective-permute-start | bytes 1493000 | tf_op jit(solution)/shard_map/ppermute | solution.py:106
  126.7 13.7 %collective-permute-start.11 = (bf16[27,24,384]{2,1,0:T(8,128)(2,1)S(1)}, bf16[27,24,384]{2,1,0:T(8,128)(2,1)S(1)}, u32[]{:S(2)}, u32[]{:S(2)}) collective-permute-start(bf16[27,24,384]{2,1,0:T(8,128)(2,1)S(1)} %collective-permute-done.9), channel_id=1, source_target_pairs={{0,1},{1,2},{2,3},{3,4},{4,5},{5,6},{6,7},{7,8},{8,9},{9,10},{10,1... | collective-permute-start | bytes 1493000 | tf_op jit(solution)/shard_map/ppermute | solution.py:101
  130.0 13.0 %collective-permute-start.12 = (bf16[27,24,384]{2,1,0:T(8,128)(2,1)S(1)}, bf16[27,24,384]{2,1,0:T(8,128)(2,1)S(1)}, u32[]{:S(2)}, u32[]{:S(2)}) collective-permute-start(bf16[27,24,384]{2,1,0:T(8,128)(2,1)S(1)} %collective-permute-done.10), channel_id=1, source_target_pairs={{0,15},{1,0},{2,1},{3,2},{4,3},{5,4},{6,5},{7,6},{8,7},{9,8},{10,9... | collective-permute-start | bytes 1493000 | tf_op jit(solution)/shard_map/ppermute | solution.py:106
  140.3 13.7 %collective-permute-start.13 = (bf16[27,24,384]{2,1,0:T(8,128)(2,1)S(1)}, bf16[27,24,384]{2,1,0:T(8,128)(2,1)S(1)}, u32[]{:S(2)}, u32[]{:S(2)}) collective-permute-start(bf16[27,24,384]{2,1,0:T(8,128)(2,1)S(1)} %collective-permute-done.11), channel_id=1, source_target_pairs={{0,1},{1,2},{2,3},{3,4},{4,5},{5,6},{6,7},{7,8},{8,9},{9,10},{10,1... | collective-permute-start | bytes 1493000 | tf_op jit(solution)/shard_map/ppermute | solution.py:101
  143.0 13.6 %collective-permute-start.14 = (bf16[27,24,384]{2,1,0:T(8,128)(2,1)S(1)}, bf16[27,24,384]{2,1,0:T(8,128)(2,1)S(1)}, u32[]{:S(2)}, u32[]{:S(2)}) collective-permute-start(bf16[27,24,384]{2,1,0:T(8,128)(2,1)S(1)} %collective-permute-done.12), channel_id=1, source_target_pairs={{0,15},{1,0},{2,1},{3,2},{4,3},{5,4},{6,5},{7,6},{8,7},{9,8},{10,9... | collective-permute-start | bytes 1493000 | tf_op jit(solution)/shard_map/ppermute | solution.py:106
  154.0 8.3 %collective-permute-start.15 = (bf16[27,24,384]{2,1,0:T(8,128)(2,1)S(1)}, bf16[27,24,384]{2,1,0:T(8,128)(2,1)S(1)}, u32[]{:S(2)}, u32[]{:S(2)}) collective-permute-start(bf16[27,24,384]{2,1,0:T(8,128)(2,1)S(1)} %collective-permute-done.13), channel_id=1, source_target_pairs={{0,1},{1,2},{2,3},{3,4},{4,5},{5,6},{6,7},{7,8},{8,9},{9,10},{10,1... | collective-permute-start | bytes 1493000 | tf_op jit(solution)/shard_map/ppermute | solution.py:101
  180.1 17.0 %copy-start.16 = (f32[384]{0:T(512)S(1)}, f32[384]{0:T(512)}, u32[]{:S(2)}) copy-start(f32[384]{0:T(512)} %param.13) | copy-start | bytes 4612
  (11 other events, 47.7 us)
